TPU v7x, 32 devices: a whole 2x2x4 slice. The times are simulated.
32 devices in a mesh: groups: 2 (over y), leaf: 4 (over z), sub: 4 (over x, core).
Axes of the slice: x: 2, y: 2, z: 4, core: 2. Of those that a mesh axis runs over, the one named last changes fastest.
Arguments:
- features: bfloat16 [512, 8192], P(('groups', 'leaf'), 'sub'), parts along dimension 0, may hold values from -6 to 6
- occupancy: int32 [512, 256], P(('groups', 'leaf'), 'sub'), parts along dimension 0, may hold values 0 or 1
- offsets: int32 [512, 13], P(('groups', 'leaf')), parts along dimension 0, may hold values from 1 to 64, as said below
- counts: int32 [512], P(('groups', 'leaf')), parts along dimension 0, may hold values from 1 to 13, as said below
- right_side: float32 [512, 256], P(('groups', 'leaf'), 'sub'), parts along dimension 0, may hold values from -3 to 8
Outputs:
- solution_field: float32 [512, 256], P(('groups', 'leaf'), 'sub'), parts along dimension 0
- residual: float32 [512, 256], P(('groups', 'leaf'), 'sub'), parts along dimension 0
There are 2 independent parts, one for each index of `groups`. A program takes and returns all parts, laid end to end along the dimension named above; each array names one. Nothing has to cross between parts.
Inputs may be any that keep to these rules, and one draw needn't show every extreme that they name: `offsets`: every offset is at least 1 and at most 64; some offset equals 64. `counts`: some leaf uses all 13 slots and some leaf uses one.
All inputs are finite; a program needn't handle non-finite values. No bound on the sum of `occupancy` on one device may be relied on, other than what follows from the above.
Results may differ from a plain program's by a relative error of at most 0.0003.
Values may be sent and summed in bfloat16 or wider, within the bound.
A program may use at most 192 MiB of HBM per device.

v0:
```python
import functools

import jax
import jax.numpy as jnp
from jax import lax
from jax.experimental import pallas as pl
from jax.experimental.pallas import tpu as pltpu
from jax.sharding import PartitionSpec as P

ITERS = 3
GROUP = 32
LANES = 128
VMEM_LIMIT = 48 * 1024 * 1024
diag_shift = 0.25
MESH = pl.DeviceIdType.MESH


def pack(x):
    k = max(1, LANES // x.shape[1])
    rows = x.shape[0] // k
    return jnp.concatenate([x[i * rows:(i + 1) * rows] for i in range(k)], axis=1)


def unpack(x, share):
    return jnp.concatenate([x[:, i:i + share] for i in range(0, x.shape[1], share)], axis=0)


def packed_shape(leaves, share):
    k = max(1, LANES // share)
    return (leaves // k, share * k)


def apply_kernel(with_ones, rows_at, cols_at, mirror_at, groups_ref, row_ref, col_ref, row_w_ref, col_w_ref, u_ref, v_ref,
                 fwd_ref, mir_ref, u_wide, v_scaled, fwd_acc, mir_acc):
    leaves, share = u_ref.shape
    voxels = v_ref.shape[1]
    count = fwd_ref.shape[0]
    row_w = row_w_ref[...]
    col_w = col_w_ref[...]
    u_wide[0] = jnp.broadcast_to((u_ref[...] * row_w)[:, :, None], u_wide.shape[1:])
    v_scaled[0] = v_ref[...] * col_w
    if with_ones:
        u_wide[1] = jnp.broadcast_to(row_w[:, :, None], u_wide.shape[1:])
        v_scaled[1] = col_w
    fwd_acc[...] = jnp.zeros_like(fwd_acc)
    mir_acc[...] = jnp.zeros_like(mir_acc)

    def fold_lanes(x):
        return sum(x[:, i:i + LANES] for i in range(0, voxels, LANES))

    def fold_rows(x):
        return sum(x[i:i + 8, :] for i in range(0, share, 8))

    def group(g, carry):
        marks, blocks = [], []
        for i in range(GROUP):
            at = g * GROUP + i
            marks.append((rows_at[at], cols_at[at], mirror_at[at]))
        for row, col, mir in marks:
            blocks.append(jnp.exp(jnp.dot(
                row_ref[jnp.minimum(row, leaves - 1)], col_ref[col],
                preferred_element_type=jnp.float32,
            )))
        for (row, col, mir), block in zip(marks, blocks):
            row_read = jnp.minimum(row, leaves - 1)
            for n in range(count):
                wide = jnp.concatenate([u_wide[n, row_read]] * (voxels // LANES), axis=1)
                fwd_acc[n, row] += fold_lanes(block * v_scaled[n, pl.ds(col, 1), :])
                mir_acc[n, mir] += fold_rows(block * wide)
        return carry

    lax.fori_loop(0, groups_ref[0], group, 0)
    for n in range(count):
        fwd_ref[n] = jnp.sum(fwd_acc[n, :leaves], axis=-1) * row_w
        mir_ref[n] = jnp.sum(mir_acc[n, :2 * leaves], axis=1) * col_w


def apply_blocks(with_ones, lists, feats, u, v):
    leaves, share = u.shape
    voxels = v.shape[1]
    count = 2 if with_ones else 1
    smem = pl.BlockSpec(memory_space=pltpu.SMEM)
    vmem = pl.BlockSpec(memory_space=pltpu.VMEM)
    return pl.pallas_call(
        functools.partial(apply_kernel, with_ones),
        out_shape=(
            jax.ShapeDtypeStruct((count, leaves, share), jnp.float32),
            jax.ShapeDtypeStruct((count, 2 * leaves, voxels), jnp.float32),
        ),
        in_specs=[smem] * 4 + [vmem] * 6,
        out_specs=(vmem, vmem),
        scratch_shapes=[
            pltpu.VMEM((count, leaves, share, LANES), jnp.float32),
            pltpu.VMEM((count, 2 * leaves, voxels), jnp.float32),
            pltpu.VMEM((count, leaves + 1, share, LANES), jnp.float32),
            pltpu.VMEM((count, 2 * leaves + 1, 8, voxels), jnp.float32),
        ],
        compiler_params=pltpu.CompilerParams(vmem_limit_bytes=VMEM_LIMIT),
    )(*lists, *feats, u, v)


def gather_kernel(n_leaf, n_sub, slab_ref, field_ref, own_out, ahead_out, window_out,
                  field_own, field_ahead, send_sem, recv_sem, field_send, field_recv):
    group_at = lax.axis_index("groups")
    leaf_at = lax.axis_index("leaf")
    sub_at = lax.axis_index("sub")
    inner = 2 if n_sub % 2 == 0 else 1
    n_out = n_sub // inner
    out_at = sub_at // inner
    in_at = sub_at % inner
    leaves, share = field_ref.shape
    behind = lax.rem(leaf_at + n_leaf - 1, n_leaf)
    devices = n_leaf * n_sub

    barrier = pltpu.get_barrier_semaphore()

    def greet(k, carry):
        to = (
            group_at,
            lax.rem(leaf_at + k // n_sub, n_leaf),
            lax.rem(sub_at + k % n_sub, n_sub),
        )
        pl.semaphore_signal(barrier, inc=1, device_id=to, device_id_type=MESH)
        return carry

    lax.fori_loop(1, devices, greet, 0)
    field_own[0] = pack(field_ref[...])
    pl.semaphore_wait(barrier, devices - 1)

    sent = []

    def send(src, dst, slot, leaf, sub):
        c = pltpu.make_async_remote_copy(
            src_ref=src, dst_ref=dst, send_sem=send_sem.at[len(sent)], recv_sem=recv_sem.at[slot],
            device_id=(group_at, leaf, sub), device_id_type=MESH,
        )
        c.start()
        sent.append(c)

    def arrived(dst, slot):
        pltpu.make_async_remote_copy(
            src_ref=slab_ref, dst_ref=dst, send_sem=send_sem.at[0], recv_sem=recv_sem.at[slot],
            device_id=(group_at, leaf_at, sub_at), device_id_type=MESH,
        ).wait_recv()

    def sub_of(outer_by, other):
        return lax.rem(out_at + outer_by, n_out) * inner + (inner - 1 - in_at if other else in_at)

    partner = sub_of(0, True)
    send(slab_ref, ahead_out.at[sub_at], n_sub + sub_at, behind, sub_at)
    for d in range(1, n_out):
        send(slab_ref, own_out.at[sub_at], sub_at, leaf_at, sub_of(d, False))
    if inner == 2:
        send(slab_ref, own_out.at[sub_at], sub_at, leaf_at, partner)
    field_copies = []
    for s in range(n_sub):
        to = lax.rem(sub_at + s, n_sub)
        field_copies.append(pltpu.make_async_remote_copy(
            src_ref=field_own.at[0], dst_ref=field_ahead.at[s],
            send_sem=field_send.at[s], recv_sem=field_recv.at[s],
            device_id=(group_at, behind, to), device_id_type=MESH,
        ))
        if s:
            field_copies.append(pltpu.make_async_remote_copy(
                src_ref=field_own.at[0], dst_ref=field_own.at[s],
                send_sem=field_send.at[n_sub + s], recv_sem=field_recv.at[n_sub + s],
                device_id=(group_at, leaf_at, to), device_id_type=MESH,
            ))
    for c in field_copies:
        c.start()
    own_out[sub_at] = slab_ref[...]
    arrived(ahead_out.at[sub_at], n_sub + sub_at)
    for d in range(1, n_out):
        send(ahead_out.at[sub_at], ahead_out.at[sub_at], n_sub + sub_at, leaf_at, sub_of(d, False))
    if inner == 2:
        send(ahead_out.at[sub_at], ahead_out.at[sub_at], n_sub + sub_at, leaf_at, partner)
    for base, out in ((0, own_out), (n_sub, ahead_out)):
        for d in range(1, n_out):
            slot = sub_of(n_out - d, False)
            arrived(out.at[slot], base + slot)
            if inner == 2:
                send(out.at[slot], out.at[slot], base + slot, leaf_at, partner)
    for c in field_copies:
        c.wait()
    for part, held in enumerate((field_own, field_ahead)):
        window_out[part * leaves:(part + 1) * leaves, :] = jnp.concatenate(
            [unpack(held[lax.rem(sub_at - s + n_sub, n_sub)], share) for s in range(n_sub)], axis=1
        )
    if inner == 2:
        for base, out in ((0, own_out), (n_sub, ahead_out)):
            for d in range(n_out):
                slot = sub_of(n_out - d, True)
                arrived(out.at[slot], base + slot)
    for c in sent:
        c.wait_send()


def gather_all(slab, field):
    n_leaf, n_sub = lax.axis_size("leaf"), lax.axis_size("sub")
    leaves, share = field.shape
    vmem = pl.BlockSpec(memory_space=pltpu.VMEM)
    slabs = jax.ShapeDtypeStruct((n_sub,) + slab.shape, slab.dtype)
    return pl.pallas_call(
        functools.partial(gather_kernel, n_leaf, n_sub),
        out_shape=(slabs, slabs, jax.ShapeDtypeStruct((2 * leaves, share * n_sub), jnp.float32)),
        in_specs=[vmem] * 2,
        out_specs=(vmem,) * 3,
        scratch_shapes=[
            pltpu.VMEM((n_sub,) + packed_shape(leaves, share), jnp.float32),
            pltpu.VMEM((n_sub,) + packed_shape(leaves, share), jnp.float32),
            pltpu.SemaphoreType.DMA((3 * n_sub + 2,)),
            pltpu.SemaphoreType.DMA((2 * n_sub,)),
            pltpu.SemaphoreType.DMA((2 * n_sub,)),
            pltpu.SemaphoreType.DMA((2 * n_sub,)),
        ],
        compiler_params=pltpu.CompilerParams(
            collective_id=ITERS, has_side_effects=True, vmem_limit_bytes=VMEM_LIMIT
        ),
    )(slab, field)


def update_kernel(first, last, n_leaf, n_sub, *refs):
    refs = list(refs)
    fwd_ref, mir_ref, occ_ref, dir_ref = refs[:4]
    del refs[:4]
    if first:
        window_ref = refs.pop(0)
        out_refs = refs[:8]
        del refs[:8]
        x_out, res_out, dir_out, u_out, win_dir_out, win_res_out, diag_out, occ_out = out_refs
    else:
        diag_ref, x_ref, res_ref = refs[:3]
        del refs[:3]
        if last:
            x_out, res_out = refs[:2]
            del refs[:2]
        else:
            win_dir_ref, win_res_ref = refs[:2]
            x_out, res_out, dir_out, u_out, win_dir_out, win_res_out = refs[2:8]
            del refs[:8]
    mir_send, mir_own, mir_back, img_own, img_ahead, scalars, send_sem, recv_sem = refs

    group_at = lax.axis_index("groups")
    leaf_at = lax.axis_index("leaf")
    sub_at = lax.axis_index("sub")
    devices = n_leaf * n_sub
    leaves, share = fwd_ref.shape[1:]
    voxels = share * n_sub
    count = fwd_ref.shape[0]

    def peer(leaf_by, sub_by):
        return (
            group_at,
            lax.rem(leaf_at + leaf_by, n_leaf),
            lax.rem(sub_at + sub_by, n_sub),
        )

    barrier = pltpu.get_barrier_semaphore()

    def greet(k, carry):
        pl.semaphore_signal(barrier, inc=1, device_id=peer(k // n_sub, k % n_sub), device_id_type=MESH)
        return carry

    lax.fori_loop(1, devices, greet, 0)
    for s in range(n_sub):
        for n in range(count):
            for part in range(2):
                mir_send[s, part, n] = pack(
                    mir_ref[n, part * leaves:(part + 1) * leaves, s * share:(s + 1) * share]
                )
    pl.semaphore_wait(barrier, devices - 1)

    def copy(src, dst, sem, leaf_by, sub_by):
        return pltpu.make_async_remote_copy(
            src_ref=src, dst_ref=dst, send_sem=send_sem.at[sem], recv_sem=recv_sem.at[sem],
            device_id=peer(leaf_by, sub_by), device_id_type=MESH,
        )

    copies = []
    for s in range(n_sub):
        to = lax.rem(sub_at + s, n_sub)
        copies.append(copy(mir_send.at[to, 1], mir_back.at[s], s, 1, s))
        copies[-1].start()
    for s in range(1, n_sub):
        to = lax.rem(sub_at + s, n_sub)
        copies.append(copy(mir_send.at[to, 0], mir_own.at[s], n_sub + s, 0, s))
        copies[-1].start()
    total = [pack(fwd_ref[n]) + mir_send[sub_at, 0, n] for n in range(count)]
    for c in copies:
        c.wait()
    for n in range(count):
        for s in range(1, n_sub):
            total[n] += mir_own[s, n]
        for s in range(n_sub):
            total[n] += mir_back[s, n]
    occ = occ_ref[...]
    direction = dir_ref[...]
    if first:
        occ = pack(occ)
        direction = pack(direction)
        occ_out[...] = occ
    if first:
        diagonal = diag_shift + total[1] / voxels
        residual = direction
        field = jnp.zeros_like(direction)
        diag_out[...] = diagonal
    else:
        diagonal = diag_ref[...]
        residual = res_ref[...]
        field = x_ref[...]
    image = diagonal * direction + occ * total[0] / voxels
    sums = (residual * residual, direction * image, residual * image, image * image)
    for i, term in enumerate(sums):
        scalars[0, i:i + 1, :] = jnp.sum(term, axis=0, keepdims=True)

    def tell(k, carry):
        copy(scalars.at[0], scalars.at[k], 4 * n_sub, k // n_sub, k % n_sub).start()
        return carry

    lax.fori_loop(1, devices, tell, 0)
    copies = []
    if not last:
        img_own[0] = occ * image
        for s in range(n_sub):
            copies.append(copy(img_own.at[0], img_ahead.at[s], 2 * n_sub + s, n_leaf - 1, s))
            copies[-1].start()
        for s in range(1, n_sub):
            copies.append(copy(img_own.at[0], img_own.at[s], 3 * n_sub + s, 0, s))
            copies[-1].start()
    everyone = copy(scalars.at[1:], scalars.at[1:], 4 * n_sub, 1, 0)
    everyone.wait()
    sums = jnp.sum(scalars[...], axis=0)
    sums = jnp.sum(sums, axis=1, keepdims=True)
    rr, dq, rq, qq = [sums[i:i + 1] for i in range(4)]
    step = rr / dq
    new = rr - 2.0 * step * rq + step * step * qq
    beta = new / rr
    field = field + step * direction
    residual = residual - step * image
    if last:
        x_out[...] = unpack(field, share)
        res_out[...] = unpack(residual, share)
        return
    x_out[...] = field
    res_out[...] = residual
    direction = residual + beta * direction
    dir_out[...] = direction
    u_out[...] = unpack(occ * direction, share)
    for c in copies:
        c.wait()
    if first:
        win_dir_ref = win_res_ref = window_ref
    for part, held in enumerate((img_own, img_ahead)):
        image_window = jnp.concatenate(
            [unpack(held[lax.rem(sub_at - s + n_sub, n_sub)], share) for s in range(n_sub)], axis=1
        )
        rows = slice(part * leaves, (part + 1) * leaves)
        res_window = win_res_ref[rows, :] - step * image_window
        win_res_out[rows, :] = res_window
        win_dir_out[rows, :] = res_window + beta * win_dir_ref[rows, :]


def update(first, last, collective_id, args):
    n_leaf, n_sub = lax.axis_size("leaf"), lax.axis_size("sub")
    count = 2 if first else 1
    leaves, share = args[0].shape[1:]
    voxels = share * n_sub
    shape = packed_shape(leaves, share)
    packed = jax.ShapeDtypeStruct(shape, jnp.float32)
    own = jax.ShapeDtypeStruct((leaves, share), jnp.float32)
    window = jax.ShapeDtypeStruct((2 * leaves, voxels), jnp.float32)
    out_shape = (own, own) if last else (packed, packed, packed, own, window, window)
    if first:
        out_shape = out_shape + (packed, packed)
    vmem = pl.BlockSpec(memory_space=pltpu.VMEM)
    return pl.pallas_call(
        functools.partial(update_kernel, first, last, n_leaf, n_sub),
        out_shape=out_shape,
        in_specs=[vmem] * len(args),
        out_specs=(vmem,) * len(out_shape),
        scratch_shapes=[
            pltpu.VMEM((n_sub, 2, count) + shape, jnp.float32),
            pltpu.VMEM((n_sub, count) + shape, jnp.float32),
            pltpu.VMEM((n_sub, count) + shape, jnp.float32),
            pltpu.VMEM((n_sub,) + shape, jnp.float32),
            pltpu.VMEM((n_sub,) + shape, jnp.float32),
            pltpu.VMEM((n_leaf * n_sub, 4, shape[1]), jnp.float32),
            pltpu.SemaphoreType.DMA((4 * n_sub + 1,)),
            pltpu.SemaphoreType.DMA((4 * n_sub + 1,)),
        ],
        compiler_params=pltpu.CompilerParams(
            collective_id=collective_id, has_side_effects=True, vmem_limit_bytes=VMEM_LIMIT
        ),
    )(*args)


def block_lists(offsets, counts):
    leaves, slots = offsets.shape
    total_leaves = leaves * lax.axis_size("leaf")
    anchor = jnp.arange(leaves, dtype=jnp.int32)[:, None]
    target = anchor + offsets
    slot_idx = jnp.arange(slots, dtype=jnp.int32)[None, :]
    usable = (slot_idx < counts[:, None]) & (target + lax.axis_index("leaf") * leaves < total_leaves)
    used = jnp.concatenate([jnp.ones((leaves, 1), bool), usable], axis=1).reshape(-1)
    cols = jnp.concatenate([anchor, target], axis=1).reshape(-1)
    rows = jnp.broadcast_to(anchor, (leaves, slots + 1)).reshape(-1)
    mirrors = jnp.concatenate([jnp.full((leaves, 1), 2 * leaves, jnp.int32), target], axis=1).reshape(-1)
    size = rows.shape[0]
    idx = jnp.arange(size, dtype=jnp.int32)
    used_i = used.astype(jnp.int32)
    before = jnp.sum(jnp.where(idx[None, :] < idx[:, None], used_i[None, :], 0), axis=1)
    length = -(-size // GROUP) * GROUP
    place = jnp.arange(length, dtype=jnp.int32)
    hit = (before[None, :] == place[:, None]) & used[None, :]
    any_hit = jnp.sum(hit.astype(jnp.int32), axis=1)

    def compact(values, fill):
        return jnp.sum(jnp.where(hit, values[None, :], 0), axis=1) + (1 - any_hit) * fill

    count = jnp.sum(used_i)
    return (
        compact(rows, leaves),
        compact(cols, 0),
        compact(mirrors, 2 * leaves),
        ((count + GROUP - 1) // GROUP).reshape((1,)),
    )


def body(features, occupancy, offsets, counts, right_side):
    leaves, share = right_side.shape
    n_sub = lax.axis_size("sub")
    voxels = share * n_sub
    feat = features.shape[1] * n_sub // voxels
    occ = occupancy.astype(jnp.float32)
    masked = occ * right_side
    part = feat // n_sub
    slab = features.reshape((leaves, part, voxels)).reshape((leaves * part, voxels))
    own_slabs, ahead_slabs, window = gather_all(slab, masked)
    lists = block_lists(offsets, counts)
    col_feat = jnp.concatenate([own_slabs, ahead_slabs]).reshape((2, n_sub, leaves, part, voxels))
    col_feat = col_feat.transpose((0, 2, 1, 3, 4)).reshape((2 * leaves, feat, voxels))
    scale = 1.0 / (2.0 * feat)
    col_w = jnp.exp(-scale * jnp.sum(jnp.square(col_feat.astype(jnp.float32)), axis=1))
    start = lax.axis_index("sub") * share
    own_rows = lax.dynamic_slice_in_dim(col_feat[:leaves], start, share, 2)
    row_w = lax.dynamic_slice_in_dim(col_w[:leaves], start, share, 1)
    row_feat = own_rows.transpose((0, 2, 1)) * jnp.bfloat16(2.0 * scale)
    feats = (row_feat, col_feat, row_w, col_w)

    fwd, mir = apply_blocks(True, lists, feats, masked, window)
    x, res, direction, u, win_dir, win_res, diagonal, occ = update(
        True, False, 0, (fwd, mir, occ, right_side, window)
    )
    for it in range(1, ITERS):
        fwd, mir = apply_blocks(False, lists, feats, u, win_dir)
        args = (fwd, mir, occ, direction, diagonal, x, res)
        if it == ITERS - 1:
            x, res = update(False, True, it, args)
        else:
            x, res, direction, u, win_dir, win_res = update(
                False, False, it, args + (win_dir, win_res)
            )
    return x, res


def solution(mesh):
    in_specs = (
        P(("groups", "leaf"), "sub"),
        P(("groups", "leaf"), "sub"),
        P(("groups", "leaf"), None),
        P(("groups", "leaf")),
        P(("groups", "leaf"), "sub"),
    )
    out_specs = (P(("groups", "leaf"), "sub"), P(("groups", "leaf"), "sub"))
    return jax.shard_map(body, mesh=mesh, in_specs=in_specs, out_specs=out_specs, check_vma=False)
```

profile of v0, /device:TPU:0, one launch (start us, length us, event | category | flops | bytes accessed | tf_op | source)
XLA Modules:
  0.0 107.9 jit_solution(4155417899763851641)
XLA Ops:
  0.6 0.7 fusion.1
  1.4 0.6 convert_reduce_fusion.1
  2.7 0.1 copy.23
  2.8 0.1 concatenate.12.clone
  2.9 0.2 reshape.34
  3.0 0.2 select_reduce_fusion.3
  3.3 0.7 iota_add_fusion
  4.0 0.1 copy.20
  4.1 0.1 concatenate.14.clone
  4.1 0.1 broadcast_in_dim.58
  4.3 0.1 copy.15
  4.4 0.1 broadcast_in_dim.56
  4.5 0.8 convert_multiply_fusion.field_ref.u_ref
  5.3 0.8 convert_element_type.23.refs_2_
  6.1 0.1 broadcast_in_dim.54
  6.2 1.8 %select_reduce_fusion = (s32[896]{0:T(1024)S(1)}, s32[896]{0:T(1024)S(1)}, s32[896]{0:T(1024)S(1)}, s32[896]{0:T(1024)S(1)}) fusion(s32[896]{0:T(1024)S(1)} %broadcast_in_dim.58, s32[896]{0:T(1024)S(1)} %select_reduce_fusion.3, pred[896]{0:T(1024)(128)(4,1)S(1)} %reshape.34, s32[896]{0:T(1024)S(1)} %broadcast_in_dim.56, s32[896]{0:T(1024)S(1)} %broadcast_in_dim.54), kind=kLoop, calls=%fused_computation.1 | loop fusion | flops 8024576 | bytes 29568 | tf_op jit(solution)/shard_map/reduce_sum | solution.py:418
  8.0 1.1 reshape_reshape.3.slab_ref
  9.1 21.9 %shard_map.68 = (bf16[4,512,256]{2,1,0:T(8,128)(2,1)S(1)}, bf16[4,512,256]{2,1,0:T(8,128)(2,1)S(1)}, f32[128,256]{1,0:T(8,128)S(1)}) custom-call(bf16[512,256]{1,0:T(8,128)(2,1)S(1)} %reshape_reshape.3.slab_ref, f32[64,64]{1,0:T(8,128)S(1)} %convert_multiply_fusion.field_ref.u_ref), custom_call_target="tpu_custom_call" | custom-call | tf_op jit(solution)/shard_map/pallas_call | solution.py:203
  31.0 0.2 pad_maximum_fusion
  31.2 0.8 multiply_reduce_fusion
  32.1 0.3 copy.25
  32.4 0.1 dynamic-slice_bitcast_fusion.row_w_ref
  32.5 0.1 slice_bitcast_fusion
  32.6 1.0 constant_dynamic-slice_fusion
  33.6 1.5 %copy.19 = bf16[64,32,64]{1,2,0:T(8,128)(2,1)S(1)} copy(bf16[64,32,64]{2,1,0:T(8,128)(2,1)} %constant_dynamic-slice_fusion) | data formatting | bytes 524288
  35.1 0.1 multiply_bitcast_fusion.row_ref
  35.2 0.0 copy-start
  35.2 15.9 %shard_map.69 = (f32[2,64,64]{2,1,0:T(8,128)S(1)}, f32[2,128,256]{2,1,0:T(8,128)S(1)}) custom-call(s32[896]{0:T(1024)S(1)} %get-tuple-element.53.rows_at, s32[896]{0:T(1024)S(1)} %get-tuple-element.47.cols_at, s32[896]{0:T(1024)S(1)} %get-tuple-element.52.mirror_at, s32[1]{0:T(128)} %bitcast.groups_ref, ...), custom_call_target="tpu_custom_call" | custom-call | tf_op jit(solution)/shard_map/pallas_call | solution.py:84
  51.1 0.0 copy-done
  51.1 12.6 %shard_map.70 = (f32[32,128]{1,0:T(8,128)S(1)}, f32[32,128]{1,0:T(8,128)S(1)}, f32[32,128]{1,0:T(8,128)S(1)}, f32[64,64]{1,0:T(8,128)S(1)}, f32[128,256]{1,0:T(8...) custom-call(f32[2,64,64]{2,1,0:T(8,128)S(1)} %get-tuple-element.27.refs_0_, ...), custom_call_target="tpu_custom_call" | custom-call | tf_op jit(solution)/shard_map/pallas_call | solution.py:376
  63.7 10.2 %shard_map.71 = (f32[1,64,64]{2,1,0:T(8,128)S(1)}, f32[1,128,256]{2,1,0:T(8,128)S(1)}) custom-call(s32[896]{0:T(1024)S(1)} %get-tuple-element.53.rows_at, s32[896]{0:T(1024)S(1)} %get-tuple-element.47.cols_at, s32[896]{0:T(1024)S(1)} %get-tuple-element.52.mirror_at, s32[1]{0:T(128)} %bitcast.groups_ref, ...), custom_call_target="tpu_custom_call" | custom-call | tf_op jit(solution)/shard_map/pallas_call | solution.py:84
  73.9 11.8 %shard_map.72 = (f32[32,128]{1,0:T(8,128)S(1)}, f32[32,128]{1,0:T(8,128)S(1)}, f32[32,128]{1,0:T(8,128)S(1)}, f32[64,64]{1,0:T(8,128)S(1)}, f32[128,256]{1,0:T(8,128)S(1)}, /*index=5*/f32[128,256]{1,0:T(8,128)}) custom-call(f32[1,64,64]{2,1,0:T(8,128)S(1)} %get-tuple-element.31.refs_0_, f32[1,128,256]{2,1,0:T(8,128)S(1)} %get-tuple-element.32.refs_1_, ...), custom_call_target="tpu_custom_call" | custom-call | tf_op jit(solution)/shard_map/pallas_call | solution.py:376
  85.7 10.0 %shard_map.73 = (f32[1,64,64]{2,1,0:T(8,128)S(1)}, f32[1,128,256]{2,1,0:T(8,128)S(1)}) custom-call(s32[896]{0:T(1024)S(1)} %get-tuple-element.53.rows_at, s32[896]{0:T(1024)S(1)} %get-tuple-element.47.cols_at, s32[896]{0:T(1024)S(1)} %get-tuple-element.52.mirror_at, s32[1]{0:T(128)} %bitcast.groups_ref, ...), custom_call_target="tpu_custom_call" | custom-call | tf_op jit(solution)/shard_map/pallas_call | solution.py:84
  95.7 11.0 %shard_map.74 = (f32[64,64]{1,0:T(8,128)S(1)}, f32[64,64]{1,0:T(8,128)S(1)}) custom-call(f32[1,64,64]{2,1,0:T(8,128)S(1)} %get-tuple-element.41.refs_0_, f32[1,128,256]{2,1,0:T(8,128)S(1)} %get-tuple-element.42.refs_1_, f32[32,128]{1,0:T(8,128)S(1)} %get-tuple-element.33.refs_2_, f32[32,128]{1,0:T(8,128)S(1)} %get-tuple-element.43.refs_3_, ...), custom_call_target="tpu_custom_call" | custom-call | tf_op jit(solution)/shard_map/pallas_call | solution.py:376
  106.7 0.6 copy.28
  107.3 0.6 copy.29
  (7 shorter events, 0.1 us)
Async XLA Ops:
  35.2 15.9 %copy-start = (f32[64,64]{1,0:T(8,128)S(1)}, f32[64,64]{1,0:T(8,128)}, u32[]{:S(2)}) copy-start(f32[64,64]{1,0:T(8,128)} %refs_3_.1) | copy-start | bytes 49156
where the time goes:
time: 108 us
  Pallas kernels  93.3 us (86%)
  other arithmetic  6.81 us (6%)
  local copies, waits for them, and re-layouts  6.28 us (6%)
  between operations  1.48 us (1%)
    pallas_call x3, Pallas kernels, apply_blocks(): pl.pallas_call(functools.partial(apply_kernel, with_ones), out_shape=(jax...  36 us
    pallas_call x3, Pallas kernels, update(): pl.pallas_call(functools.partial(update_kernel, first, last, n_leaf, n_su...  35.4 us
    pallas_call x1, Pallas kernels, gather_all(): pl.pallas_call(functools.partial(gather_kernel, n_leaf, n_sub), out_shape...  21.9 us
    unnamed x7, local copies, waits for them, and re-layouts  2.95 us

commit v1 on v0

--- a/solution.py
+++ b/solution.py
@@ -30,7 +30,7 @@
     return (leaves // k, share * k)
 
 
-def apply_kernel(with_ones, rows_at, cols_at, mirror_at, groups_ref, row_ref, col_ref, row_w_ref, col_w_ref, u_ref, v_ref,
+def apply_kernel(with_ones, codes_ref, row_ref, col_ref, row_w_ref, col_w_ref, u_ref, v_ref,
                  fwd_ref, mir_ref, u_wide, v_scaled, fwd_acc, mir_acc):
     leaves, share = u_ref.shape
     voxels = v_ref.shape[1]
@@ -55,7 +55,10 @@
         marks, blocks = [], []
         for i in range(GROUP):
             at = g * GROUP + i
-            marks.append((rows_at[at], cols_at[at], mirror_at[at]))
+            code = codes_ref[0, at]
+            row = code // (4 * leaves)
+            col = code % (4 * leaves)
+            marks.append((row, col, jnp.where(row == col, 2 * leaves, col)))
         for row, col, mir in marks:
             blocks.append(jnp.exp(jnp.dot(
                 row_ref[jnp.minimum(row, leaves - 1)], col_ref[col],
@@ -69,13 +72,13 @@
                 mir_acc[n, mir] += fold_rows(block * wide)
         return carry
 
-    lax.fori_loop(0, groups_ref[0], group, 0)
+    lax.fori_loop(0, codes_ref[0, codes_ref.shape[1] - 1], group, 0)
     for n in range(count):
         fwd_ref[n] = jnp.sum(fwd_acc[n, :leaves], axis=-1) * row_w
         mir_ref[n] = jnp.sum(mir_acc[n, :2 * leaves], axis=1) * col_w
 
 
-def apply_blocks(with_ones, lists, feats, u, v):
+def apply_blocks(with_ones, codes, feats, u, v):
     leaves, share = u.shape
     voxels = v.shape[1]
     count = 2 if with_ones else 1
@@ -87,7 +90,7 @@
             jax.ShapeDtypeStruct((count, leaves, share), jnp.float32),
             jax.ShapeDtypeStruct((count, 2 * leaves, voxels), jnp.float32),
         ),
-        in_specs=[smem] * 4 + [vmem] * 6,
+        in_specs=[smem] + [vmem] * 6,
         out_specs=(vmem, vmem),
         scratch_shapes=[
             pltpu.VMEM((count, leaves, share, LANES), jnp.float32),
@@ -96,10 +99,40 @@
             pltpu.VMEM((count, 2 * leaves + 1, 8, voxels), jnp.float32),
         ],
         compiler_params=pltpu.CompilerParams(vmem_limit_bytes=VMEM_LIMIT),
-    )(*lists, *feats, u, v)
-
-
-def gather_kernel(n_leaf, n_sub, slab_ref, field_ref, own_out, ahead_out, window_out,
+    )(codes, *feats, u, v)
+
+
+def used_blocks(offsets, counts, leaf_at, total_leaves, width):
+    leaves, slots = offsets.shape
+    row = lax.broadcasted_iota(jnp.int32, (leaves, 1), 0)
+    place = lax.broadcasted_iota(jnp.int32, (leaves, width), 1)
+    targets, used = [row], [jnp.ones((leaves, 1), jnp.int32)]
+    for j in range(slots):
+        target = row + offsets[:, j:j + 1]
+        fits = (counts > j) & (target + leaf_at * leaves < total_leaves)
+        targets.append(target)
+        used.append(fits.astype(jnp.int32))
+    row_count = sum(used).astype(jnp.float32)
+    earlier = (
+        lax.broadcasted_iota(jnp.int32, (leaves, leaves), 1)
+        < lax.broadcasted_iota(jnp.int32, (leaves, leaves), 0)
+    ).astype(jnp.float32)
+    at = jnp.dot(
+        earlier, jnp.broadcast_to(row_count, (leaves, LANES)), preferred_element_type=jnp.float32
+    )[:, :1].astype(jnp.int32)
+    filler = leaves * 4 * leaves + leaves
+    codes = jnp.zeros((leaves, width), jnp.int32)
+    for target, use in zip(targets, used):
+        hit = (place == at) & (use > 0)
+        codes = codes + jnp.where(hit, row * (4 * leaves) + target - filler, 0)
+        at = at + use
+    codes = jnp.sum(codes, axis=0, keepdims=True) + filler
+    turns = (jnp.sum(row_count, axis=0, keepdims=True).astype(jnp.int32) + (GROUP - 1)) // GROUP
+    return jnp.where(place[:1] == width - 1, turns, codes)
+
+
+def gather_kernel(n_leaf, n_sub, slab_ref, field_ref, offsets_ref, counts_ref,
+                  own_out, ahead_out, window_out, codes_out,
                   field_own, field_ahead, send_sem, recv_sem, field_send, field_recv):
     group_at = lax.axis_index("groups")
     leaf_at = lax.axis_index("leaf")
@@ -137,9 +170,11 @@
         c.start()
         sent.append(c)
 
-    def arrived(dst, slot):
+    half = slab_ref.shape[0] // 2
+
+    def arrived(dst, slot, src=slab_ref):
         pltpu.make_async_remote_copy(
-            src_ref=slab_ref, dst_ref=dst, send_sem=send_sem.at[0], recv_sem=recv_sem.at[slot],
+            src_ref=src, dst_ref=dst, send_sem=send_sem.at[0], recv_sem=recv_sem.at[slot],
             device_id=(group_at, leaf_at, sub_at), device_id_type=MESH,
         ).wait_recv()
 
@@ -169,17 +204,27 @@
     for c in field_copies:
         c.start()
     own_out[sub_at] = slab_ref[...]
+    codes_out[...] = used_blocks(
+        offsets_ref[...], counts_ref[...], leaf_at, n_leaf * leaves, codes_out.shape[1]
+    )
     arrived(ahead_out.at[sub_at], n_sub + sub_at)
+    low, high = pl.ds(0, half), pl.ds(half, half)
     for d in range(1, n_out):
-        send(ahead_out.at[sub_at], ahead_out.at[sub_at], n_sub + sub_at, leaf_at, sub_of(d, False))
+        send(ahead_out.at[sub_at, low], ahead_out.at[sub_at, low], n_sub + sub_at, leaf_at, sub_of(d, False))
+    for d in range(1, n_out):
+        slot = sub_of(n_out - d, False)
+        arrived(own_out.at[slot], slot)
+        send(own_out.at[slot, high], ahead_out.at[slot, high], 2 * n_sub + slot, behind, sub_at)
+        if inner == 2:
+            send(own_out.at[slot], own_out.at[slot], slot, leaf_at, partner)
     if inner == 2:
         send(ahead_out.at[sub_at], ahead_out.at[sub_at], n_sub + sub_at, leaf_at, partner)
-    for base, out in ((0, own_out), (n_sub, ahead_out)):
-        for d in range(1, n_out):
-            slot = sub_of(n_out - d, False)
-            arrived(out.at[slot], base + slot)
-            if inner == 2:
-                send(out.at[slot], out.at[slot], base + slot, leaf_at, partner)
+    for d in range(1, n_out):
+        slot = sub_of(n_out - d, False)
+        arrived(ahead_out.at[slot, low], n_sub + slot, slab_ref.at[low])
+        arrived(ahead_out.at[slot, high], 2 * n_sub + slot, slab_ref.at[high])
+        if inner == 2:
+            send(ahead_out.at[slot], ahead_out.at[slot], n_sub + slot, leaf_at, partner)
     for c in field_copies:
         c.wait()
     for part, held in enumerate((field_own, field_ahead)):
@@ -195,28 +240,30 @@
         c.wait_send()
 
 
-def gather_all(slab, field):
+def gather_all(slab, field, offsets, counts):
     n_leaf, n_sub = lax.axis_size("leaf"), lax.axis_size("sub")
     leaves, share = field.shape
     vmem = pl.BlockSpec(memory_space=pltpu.VMEM)
     slabs = jax.ShapeDtypeStruct((n_sub,) + slab.shape, slab.dtype)
+    length = -(-leaves * (offsets.shape[1] + 1) // LANES) * LANES
     return pl.pallas_call(
         functools.partial(gather_kernel, n_leaf, n_sub),
-        out_shape=(slabs, slabs, jax.ShapeDtypeStruct((2 * leaves, share * n_sub), jnp.float32)),
-        in_specs=[vmem] * 2,
-        out_specs=(vmem,) * 3,
+        out_shape=(slabs, slabs, jax.ShapeDtypeStruct((2 * leaves, share * n_sub), jnp.float32),
+                   jax.ShapeDtypeStruct((1, length + LANES), jnp.int32)),
+        in_specs=[vmem] * 4,
+        out_specs=(vmem,) * 4,
         scratch_shapes=[
             pltpu.VMEM((n_sub,) + packed_shape(leaves, share), jnp.float32),
             pltpu.VMEM((n_sub,) + packed_shape(leaves, share), jnp.float32),
             pltpu.SemaphoreType.DMA((3 * n_sub + 2,)),
-            pltpu.SemaphoreType.DMA((2 * n_sub,)),
+            pltpu.SemaphoreType.DMA((3 * n_sub,)),
             pltpu.SemaphoreType.DMA((2 * n_sub,)),
             pltpu.SemaphoreType.DMA((2 * n_sub,)),
         ],
         compiler_params=pltpu.CompilerParams(
             collective_id=ITERS, has_side_effects=True, vmem_limit_bytes=VMEM_LIMIT
         ),
-    )(slab, field)
+    )(slab, field, offsets, counts[:, None])
 
 
 def update_kernel(first, last, n_leaf, n_sub, *refs):
@@ -394,38 +441,6 @@
     )(*args)
 
 
-def block_lists(offsets, counts):
-    leaves, slots = offsets.shape
-    total_leaves = leaves * lax.axis_size("leaf")
-    anchor = jnp.arange(leaves, dtype=jnp.int32)[:, None]
-    target = anchor + offsets
-    slot_idx = jnp.arange(slots, dtype=jnp.int32)[None, :]
-    usable = (slot_idx < counts[:, None]) & (target + lax.axis_index("leaf") * leaves < total_leaves)
-    used = jnp.concatenate([jnp.ones((leaves, 1), bool), usable], axis=1).reshape(-1)
-    cols = jnp.concatenate([anchor, target], axis=1).reshape(-1)
-    rows = jnp.broadcast_to(anchor, (leaves, slots + 1)).reshape(-1)
-    mirrors = jnp.concatenate([jnp.full((leaves, 1), 2 * leaves, jnp.int32), target], axis=1).reshape(-1)
-    size = rows.shape[0]
-    idx = jnp.arange(size, dtype=jnp.int32)
-    used_i = used.astype(jnp.int32)
-    before = jnp.sum(jnp.where(idx[None, :] < idx[:, None], used_i[None, :], 0), axis=1)
-    length = -(-size // GROUP) * GROUP
-    place = jnp.arange(length, dtype=jnp.int32)
-    hit = (before[None, :] == place[:, None]) & used[None, :]
-    any_hit = jnp.sum(hit.astype(jnp.int32), axis=1)
-
-    def compact(values, fill):
-        return jnp.sum(jnp.where(hit, values[None, :], 0), axis=1) + (1 - any_hit) * fill
-
-    count = jnp.sum(used_i)
-    return (
-        compact(rows, leaves),
-        compact(cols, 0),
-        compact(mirrors, 2 * leaves),
-        ((count + GROUP - 1) // GROUP).reshape((1,)),
-    )
-
-
 def body(features, occupancy, offsets, counts, right_side):
     leaves, share = right_side.shape
     n_sub = lax.axis_size("sub")
@@ -435,8 +450,7 @@
     masked = occ * right_side
     part = feat // n_sub
     slab = features.reshape((leaves, part, voxels)).reshape((leaves * part, voxels))
-    own_slabs, ahead_slabs, window = gather_all(slab, masked)
-    lists = block_lists(offsets, counts)
+    own_slabs, ahead_slabs, window, codes = gather_all(slab, masked, offsets, counts)
     col_feat = jnp.concatenate([own_slabs, ahead_slabs]).reshape((2, n_sub, leaves, part, voxels))
     col_feat = col_feat.transpose((0, 2, 1, 3, 4)).reshape((2 * leaves, feat, voxels))
     scale = 1.0 / (2.0 * feat)
@@ -447,12 +461,12 @@
     row_feat = own_rows.transpose((0, 2, 1)) * jnp.bfloat16(2.0 * scale)
     feats = (row_feat, col_feat, row_w, col_w)
 
-    fwd, mir = apply_blocks(True, lists, feats, masked, window)
+    fwd, mir = apply_blocks(True, codes, feats, masked, window)
     x, res, direction, u, win_dir, win_res, diagonal, occ = update(
         True, False, 0, (fwd, mir, occ, right_side, window)
     )
     for it in range(1, ITERS):
-        fwd, mir = apply_blocks(False, lists, feats, u, win_dir)
+        fwd, mir = apply_blocks(False, codes, feats, u, win_dir)
         args = (fwd, mir, occ, direction, diagonal, x, res)
         if it == ITERS - 1:
             x, res = update(False, True, it, args)

time: 108 us -> 105 us (0.972)
  other arithmetic: 6.81 us -> 2.71 us
    pallas_call x3, Pallas kernels: 36 us -> 39.9 us  [apply_blocks(): pl.pallas_call(functools.partial(apply_kernel, with_ones), out_shape=(jax...]
    pallas_call x1, Pallas kernels: 21.9 us -> 19.2 us  [gather_all(): pl.pallas_call(functools.partial(gather_kernel, n_leaf, n_sub), out_shape...]
    reduce_sum x3 -> x0, other arithmetic: 2.68 us -> none  [the longest x1 1.83 us: compact(): jnp.sum(jnp.where(hit, values[None, :], 0), axis=1) + (1 - any_hit) * fill]
    unnamed x7 -> x6, local copies, waits for them, and re-layouts: 2.95 us -> 3.52 us
where the time goes in v1:
time: 105 us; the launch traced here: 104 us
  Pallas kernels  94.2 us (90%)
  local copies, waits for them, and re-layouts  6.79 us (6%)
  other arithmetic  2.71 us (3%)
    pallas_call x3, Pallas kernels, apply_blocks(): pl.pallas_call(functools.partial(apply_kernel, with_ones), out_shape=(jax...  39.9 us
    pallas_call x3, Pallas kernels, update(): pl.pallas_call(functools.partial(update_kernel, first, last, n_leaf, n_su...  35.1 us
    pallas_call x1, Pallas kernels, gather_all(): pl.pallas_call(functools.partial(gather_kernel, n_leaf, n_sub), out_shape...  19.2 us
    unnamed x6, local copies, waits for them, and re-layouts  3.52 us

profile of v1, /device:TPU:0, one launch (start us, length us, event | category | flops | bytes accessed | tf_op | source)
XLA Modules:
  0.0 104.5 jit_solution(5344535606393320364)
XLA Ops:
  0.6 0.8 convert_multiply_fusion.field_ref.u_ref
  1.4 0.8 copy.11.offsets_ref
  2.2 0.7 copy.12.counts_ref
  2.9 0.8 convert_element_type.7.refs_2_
  3.7 1.1 %reshape_reshape.3.slab_ref = bf16[512,256]{1,0:T(8,128)(2,1)S(1)} reshape(bf16[64,2048]{1,0:T(8,128)(2,1)} %param.5) | data formatting | bytes 524288 | tf_op jit(solution)/shard_map/reshape;reshape | solution.py:452
  4.8 19.2 %shard_map.68 = (bf16[4,512,256]{2,1,0:T(8,128)(2,1)S(1)}, bf16[4,512,256]{2,1,0:T(8,128)(2,1)S(1)}, f32[128,256]{1,0:T(8,128)S(1)}, s32[1,1024]{1,0:T(1,128)S(1)}) custom-call(bf16[512,256]{1,0:T(8,128)(2,1)S(1)} %reshape_reshape.3.slab_ref, f32[64,64]{1,0:T(8,128)S(1)} %convert_multiply_fusion.field_ref.u_ref, s32[64,13]{1,0:T(8,128)S(1)} %copy.11.offsets_ref, ...), custom_call_target="tpu_custom_call" | custom-call | tf_op jit(solution)/shard_map/pallas_call | solution.py:249
  24.0 0.2 pad_maximum_fusion
  24.2 0.9 multiply_reduce_fusion
  25.0 0.3 copy.19
  25.4 0.1 dynamic-slice_bitcast_fusion.row_w_ref
  25.4 0.1 slice_bitcast_fusion
  25.5 1.0 constant_dynamic-slice_fusion
  26.5 1.5 %copy.15 = bf16[64,32,64]{1,2,0:T(8,128)(2,1)S(1)} copy(bf16[64,32,64]{2,1,0:T(8,128)(2,1)} %constant_dynamic-slice_fusion) | data formatting | bytes 524288
  28.0 0.1 multiply_bitcast_fusion.row_ref
  28.1 0.0 copy-start
  28.1 17.3 %shard_map.69 = (f32[2,64,64]{2,1,0:T(8,128)S(1)}, f32[2,128,256]{2,1,0:T(8,128)S(1)}) custom-call(s32[1,1024]{1,0:T(1,128)S(1)} %get-tuple-element.25.codes_ref, bf16[64,64,32]{2,1,0:T(8,128)(2,1)S(1)} %multiply_bitcast_fusion.row_ref, bf16[128,32,256]{2,1,0:T(8,128)(2,1)S(1)} %bitcast.15, f32[64,64]{1,0:T(8,128)S(1)} %dynamic-slice_bitcast_fusion.row_w_ref, ...), custom_call_target="tpu_custom_call" | custom-call | tf_op jit(solution)/shard_map/pallas_call | solution.py:87
  45.4 0.0 copy-done
  45.4 12.8 %shard_map.70 = (f32[32,128]{1,0:T(8,128)S(1)}, f32[32,128]{1,0:T(8,128)S(1)}, f32[32,128]{1,0:T(8,128)S(1)}, f32[64,64]{1,0:T(8,128)S(1)}, f32[128,256]{1,0:T(8...) custom-call(f32[2,64,64]{2,1,0:T(8,128)S(1)} %get-tuple-element.29.refs_0_, ...), custom_call_target="tpu_custom_call" | custom-call | tf_op jit(solution)/shard_map/pallas_call | solution.py:423
  58.2 11.3 %shard_map.71 = (f32[1,64,64]{2,1,0:T(8,128)S(1)}, f32[1,128,256]{2,1,0:T(8,128)S(1)}) custom-call(s32[1,1024]{1,0:T(1,128)S(1)} %get-tuple-element.25.codes_ref, bf16[64,64,32]{2,1,0:T(8,128)(2,1)S(1)} %multiply_bitcast_fusion.row_ref, bf16[128,32,256]{2,1,0:T(8,128)(2,1)S(1)} %bitcast.16, f32[64,64]{1,0:T(8,128)S(1)} %dynamic-slice_bitcast_fusion.row_w_ref, ...), custom_call_target="tpu_custom_call" | custom-call | tf_op jit(solution)/shard_map/pallas_call | solution.py:87
  69.5 11.5 %shard_map.72 = (f32[32,128]{1,0:T(8,128)S(1)}, f32[32,128]{1,0:T(8,128)S(1)}, f32[32,128]{1,0:T(8,128)S(1)}, f32[64,64]{1,0:T(8,128)S(1)}, f32[128,256]{1,0:T(8,128)S(1)}, /*index=5*/f32[128,256]{1,0:T(8,128)}) custom-call(f32[1,64,64]{2,1,0:T(8,128)S(1)} %get-tuple-element.33.refs_0_, f32[1,128,256]{2,1,0:T(8,128)S(1)} %get-tuple-element.34.refs_1_, ...), custom_call_target="tpu_custom_call" | custom-call | tf_op jit(solution)/shard_map/pallas_call | solution.py:423
  81.1 11.3 %shard_map.73 = (f32[1,64,64]{2,1,0:T(8,128)S(1)}, f32[1,128,256]{2,1,0:T(8,128)S(1)}) custom-call(s32[1,1024]{1,0:T(1,128)S(1)} %get-tuple-element.25.codes_ref, bf16[64,64,32]{2,1,0:T(8,128)(2,1)S(1)} %multiply_bitcast_fusion.row_ref, bf16[128,32,256]{2,1,0:T(8,128)(2,1)S(1)} %bitcast.17, f32[64,64]{1,0:T(8,128)S(1)} %dynamic-slice_bitcast_fusion.row_w_ref, ...), custom_call_target="tpu_custom_call" | custom-call | tf_op jit(solution)/shard_map/pallas_call | solution.py:87
  92.4 10.8 %shard_map.74 = (f32[64,64]{1,0:T(8,128)S(1)}, f32[64,64]{1,0:T(8,128)S(1)}) custom-call(f32[1,64,64]{2,1,0:T(8,128)S(1)} %get-tuple-element.43.refs_0_, f32[1,128,256]{2,1,0:T(8,128)S(1)} %get-tuple-element.44.refs_1_, f32[32,128]{1,0:T(8,128)S(1)} %get-tuple-element.35.refs_2_, f32[32,128]{1,0:T(8,128)S(1)} %get-tuple-element.45.refs_3_, ...), custom_call_target="tpu_custom_call" | custom-call | tf_op jit(solution)/shard_map/pallas_call | solution.py:423
  103.3 0.6 copy.22
  103.9 0.6 copy.23
  (2 shorter events, 0.0 us)
Async XLA Ops:
  28.1 17.3 %copy-start = (f32[64,64]{1,0:T(8,128)S(1)}, f32[64,64]{1,0:T(8,128)}, u32[]{:S(2)}) copy-start(f32[64,64]{1,0:T(8,128)} %refs_3_.1) | copy-start | bytes 49156

commit v2 on v1

--- a/solution.py
+++ b/solution.py
@@ -55,10 +55,7 @@
         marks, blocks = [], []
         for i in range(GROUP):
             at = g * GROUP + i
-            code = codes_ref[0, at]
-            row = code // (4 * leaves)
-            col = code % (4 * leaves)
-            marks.append((row, col, jnp.where(row == col, 2 * leaves, col)))
+            marks.append((codes_ref[0, at], codes_ref[1, at], codes_ref[2, at]))
         for row, col, mir in marks:
             blocks.append(jnp.exp(jnp.dot(
                 row_ref[jnp.minimum(row, leaves - 1)], col_ref[col],
@@ -72,7 +69,7 @@
                 mir_acc[n, mir] += fold_rows(block * wide)
         return carry
 
-    lax.fori_loop(0, codes_ref[0, codes_ref.shape[1] - 1], group, 0)
+    lax.fori_loop(0, codes_ref[3, 0], group, 0)
     for n in range(count):
         fwd_ref[n] = jnp.sum(fwd_acc[n, :leaves], axis=-1) * row_w
         mir_ref[n] = jnp.sum(mir_acc[n, :2 * leaves], axis=1) * col_w
@@ -120,15 +117,18 @@
     at = jnp.dot(
         earlier, jnp.broadcast_to(row_count, (leaves, LANES)), preferred_element_type=jnp.float32
     )[:, :1].astype(jnp.int32)
-    filler = leaves * 4 * leaves + leaves
-    codes = jnp.zeros((leaves, width), jnp.int32)
+    rows = jnp.zeros((leaves, width), jnp.int32)
+    cols = jnp.zeros((leaves, width), jnp.int32)
     for target, use in zip(targets, used):
         hit = (place == at) & (use > 0)
-        codes = codes + jnp.where(hit, row * (4 * leaves) + target - filler, 0)
+        rows = rows + jnp.where(hit, row - leaves, 0)
+        cols = cols + jnp.where(hit, target - leaves, 0)
         at = at + use
-    codes = jnp.sum(codes, axis=0, keepdims=True) + filler
+    rows = jnp.sum(rows, axis=0, keepdims=True) + leaves
+    cols = jnp.sum(cols, axis=0, keepdims=True) + leaves
     turns = (jnp.sum(row_count, axis=0, keepdims=True).astype(jnp.int32) + (GROUP - 1)) // GROUP
-    return jnp.where(place[:1] == width - 1, turns, codes)
+    mirrors = jnp.where(rows == cols, 2 * leaves, cols)
+    return jnp.concatenate([rows, cols, mirrors, jnp.broadcast_to(turns, rows.shape)], axis=0)
 
 
 def gather_kernel(n_leaf, n_sub, slab_ref, field_ref, offsets_ref, counts_ref,
@@ -249,7 +249,7 @@
     return pl.pallas_call(
         functools.partial(gather_kernel, n_leaf, n_sub),
         out_shape=(slabs, slabs, jax.ShapeDtypeStruct((2 * leaves, share * n_sub), jnp.float32),
-                   jax.ShapeDtypeStruct((1, length + LANES), jnp.int32)),
+                   jax.ShapeDtypeStruct((4, length), jnp.int32)),
         in_specs=[vmem] * 4,
         out_specs=(vmem,) * 4,
         scratch_shapes=[

time: 105 us -> 103 us (0.981); the launches traced: 104 us -> 101 us
  Pallas kernels: 94.2 us -> 90.8 us
    pallas_call x3, Pallas kernels: 39.9 us -> 36.1 us  [apply_blocks(): pl.pallas_call(functools.partial(apply_kernel, with_ones), out_shape=(jax...]
where the time goes in v2:
time: 103 us; the launch traced here: 101 us
  Pallas kernels  90.8 us (88%)
  local copies, waits for them, and re-layouts  6.79 us (7%)
  other arithmetic  2.67 us (3%)
    pallas_call x3, Pallas kernels, apply_blocks(): pl.pallas_call(functools.partial(apply_kernel, with_ones), out_shape=(jax...  36.1 us
    pallas_call x3, Pallas kernels, update(): pl.pallas_call(functools.partial(update_kernel, first, last, n_leaf, n_su...  35.5 us
    pallas_call x1, Pallas kernels, gather_all(): pl.pallas_call(functools.partial(gather_kernel, n_leaf, n_sub), out_shape...  19.2 us
    unnamed x6, local copies, waits for them, and re-layouts  3.52 us

profile of v2, /device:TPU:0, one launch (start us, length us, event | category | flops | bytes accessed | tf_op | source)
XLA Modules:
  0.0 101.0 jit_solution(16694930303002087216)
XLA Ops:
  0.6 0.8 convert_multiply_fusion.field_ref.u_ref
  1.4 0.8 copy.11.offsets_ref
  2.2 0.7 copy.12.counts_ref
  2.9 0.8 convert_element_type.7.refs_2_
  3.7 1.1 %reshape_reshape.3.slab_ref = bf16[512,256]{1,0:T(8,128)(2,1)S(1)} reshape(bf16[64,2048]{1,0:T(8,128)(2,1)} %param.5) | data formatting | bytes 524288 | tf_op jit(solution)/shard_map/reshape;reshape | solution.py:452
  4.8 19.2 %shard_map.68 = (bf16[4,512,256]{2,1,0:T(8,128)(2,1)S(1)}, bf16[4,512,256]{2,1,0:T(8,128)(2,1)S(1)}, f32[128,256]{1,0:T(8,128)S(1)}, s32[4,896]{1,0:T(4,128)S(1)}) custom-call(bf16[512,256]{1,0:T(8,128)(2,1)S(1)} %reshape_reshape.3.slab_ref, f32[64,64]{1,0:T(8,128)S(1)} %convert_multiply_fusion.field_ref.u_ref, s32[64,13]{1,0:T(8,128)S(1)} %copy.11.offsets_ref, ...), custom_call_target="tpu_custom_call" | custom-call | tf_op jit(solution)/shard_map/pallas_call | solution.py:249
  24.0 0.2 pad_maximum_fusion
  24.2 0.8 multiply_reduce_fusion
  25.0 0.3 copy.19
  25.3 0.1 dynamic-slice_bitcast_fusion.row_w_ref
  25.4 0.1 slice_bitcast_fusion
  25.5 1.0 constant_dynamic-slice_fusion
  26.5 1.5 %copy.15 = bf16[64,32,64]{1,2,0:T(8,128)(2,1)S(1)} copy(bf16[64,32,64]{2,1,0:T(8,128)(2,1)} %constant_dynamic-slice_fusion) | data formatting | bytes 524288
  28.0 0.1 multiply_bitcast_fusion.row_ref
  28.1 0.0 copy-start
  28.1 16.1 %shard_map.69 = (f32[2,64,64]{2,1,0:T(8,128)S(1)}, f32[2,128,256]{2,1,0:T(8,128)S(1)}) custom-call(s32[4,896]{1,0:T(4,128)S(1)} %get-tuple-element.25.codes_ref, bf16[64,64,32]{2,1,0:T(8,128)(2,1)S(1)} %multiply_bitcast_fusion.row_ref, bf16[128,32,256]{2,1,0:T(8,128)(2,1)S(1)} %bitcast.15, f32[64,64]{1,0:T(8,128)S(1)} %dynamic-slice_bitcast_fusion.row_w_ref, ...), custom_call_target="tpu_custom_call" | custom-call | tf_op jit(solution)/shard_map/pallas_call | solution.py:84
  44.2 0.0 copy-done
  44.2 13.2 %shard_map.70 = (f32[32,128]{1,0:T(8,128)S(1)}, f32[32,128]{1,0:T(8,128)S(1)}, f32[32,128]{1,0:T(8,128)S(1)}, f32[64,64]{1,0:T(8,128)S(1)}, f32[128,256]{1,0:T(8...) custom-call(f32[2,64,64]{2,1,0:T(8,128)S(1)} %get-tuple-element.29.refs_0_, ...), custom_call_target="tpu_custom_call" | custom-call | tf_op jit(solution)/shard_map/pallas_call | solution.py:423
  57.3 10.0 %shard_map.71 = (f32[1,64,64]{2,1,0:T(8,128)S(1)}, f32[1,128,256]{2,1,0:T(8,128)S(1)}) custom-call(s32[4,896]{1,0:T(4,128)S(1)} %get-tuple-element.25.codes_ref, bf16[64,64,32]{2,1,0:T(8,128)(2,1)S(1)} %multiply_bitcast_fusion.row_ref, bf16[128,32,256]{2,1,0:T(8,128)(2,1)S(1)} %bitcast.16, f32[64,64]{1,0:T(8,128)S(1)} %dynamic-slice_bitcast_fusion.row_w_ref, ...), custom_call_target="tpu_custom_call" | custom-call | tf_op jit(solution)/shard_map/pallas_call | solution.py:84
  67.4 12.1 %shard_map.72 = (f32[32,128]{1,0:T(8,128)S(1)}, f32[32,128]{1,0:T(8,128)S(1)}, f32[32,128]{1,0:T(8,128)S(1)}, f32[64,64]{1,0:T(8,128)S(1)}, f32[128,256]{1,0:T(8,128)S(1)}, /*index=5*/f32[128,256]{1,0:T(8,128)}) custom-call(f32[1,64,64]{2,1,0:T(8,128)S(1)} %get-tuple-element.33.refs_0_, f32[1,128,256]{2,1,0:T(8,128)S(1)} %get-tuple-element.34.refs_1_, ...), custom_call_target="tpu_custom_call" | custom-call | tf_op jit(solution)/shard_map/pallas_call | solution.py:423
  79.5 10.0 %shard_map.73 = (f32[1,64,64]{2,1,0:T(8,128)S(1)}, f32[1,128,256]{2,1,0:T(8,128)S(1)}) custom-call(s32[4,896]{1,0:T(4,128)S(1)} %get-tuple-element.25.codes_ref, bf16[64,64,32]{2,1,0:T(8,128)(2,1)S(1)} %multiply_bitcast_fusion.row_ref, bf16[128,32,256]{2,1,0:T(8,128)(2,1)S(1)} %bitcast.17, f32[64,64]{1,0:T(8,128)S(1)} %dynamic-slice_bitcast_fusion.row_w_ref, ...), custom_call_target="tpu_custom_call" | custom-call | tf_op jit(solution)/shard_map/pallas_call | solution.py:84
  89.5 10.3 %shard_map.74 = (f32[64,64]{1,0:T(8,128)S(1)}, f32[64,64]{1,0:T(8,128)S(1)}) custom-call(f32[1,64,64]{2,1,0:T(8,128)S(1)} %get-tuple-element.43.refs_0_, f32[1,128,256]{2,1,0:T(8,128)S(1)} %get-tuple-element.44.refs_1_, f32[32,128]{1,0:T(8,128)S(1)} %get-tuple-element.35.refs_2_, f32[32,128]{1,0:T(8,128)S(1)} %get-tuple-element.45.refs_3_, ...), custom_call_target="tpu_custom_call" | custom-call | tf_op jit(solution)/shard_map/pallas_call | solution.py:423
  99.8 0.6 copy.22
  100.4 0.6 copy.23
  (2 shorter events, 0.0 us)
Async XLA Ops:
  28.1 16.1 %copy-start = (f32[64,64]{1,0:T(8,128)S(1)}, f32[64,64]{1,0:T(8,128)}, u32[]{:S(2)}) copy-start(f32[64,64]{1,0:T(8,128)} %refs_3_.1) | copy-start | bytes 49156
